TPU v7x, 32 devices: a whole 2x2x4 slice. The times are simulated.
32 devices in a mesh: groups: 2 (over x), tm: 16 (over z, y, core).
Axes of the slice: x: 2, y: 2, z: 4, core: 2. Of those that a mesh axis runs over, the one named last changes fastest.
Arguments:
- tokens: bfloat16 [2, 4096, 1152], P('groups', 'tm'), parts along dimension 0, may hold values from -6 to 6
- norm_gain: float32 [1152], replicated, may hold values from 0.5 to 8
- w_qkv: bfloat16 [1152, 1728], P('tm'), may hold values from -0.1875 to 0.1875
- w_out: bfloat16 [1152, 576], P('tm'), may hold values from -0.25 to 0.25
- block_mask: int32 [2, 2, 2], P('groups'), parts along dimension 0, may hold values from 0 to 1
- keep_tiles: int32 [2, 256], P('groups', 'tm'), parts along dimension 0, may hold values 0 or 1
- cotangent: bfloat16 [2, 4096, 1152], P('groups', 'tm'), parts along dimension 0, may hold values from -6 to 6
Outputs:
- mixed: bfloat16 [2, 4096, 1152], P('groups', 'tm'), parts along dimension 0
- grad_tokens: bfloat16 [2, 4096, 1152], P('groups', 'tm'), parts along dimension 0
- grad_qkv: float32 [2304, 1728], P(('groups', 'tm')), parts along dimension 0
- grad_out: float32 [2304, 576], P(('groups', 'tm')), parts along dimension 0
There are 2 independent parts, one for each index of `groups`. A program takes and returns all parts, laid end to end along the dimension named above; an argument that names none is the same for every part. Nothing has to cross between parts.
All inputs are finite; a program needn't handle non-finite values. No bound on the sum of `keep_tiles` on one device may be relied on, other than what follows from the above.
Results may differ from a plain program's by a relative error of at most 0.0055.
The roundings to bfloat16 on the way count: a program that leaves them out, or rounds other values in their place, can miss the bound.
Values may be sent and summed in bfloat16 or wider, within the bound.
A program may use at most 128 MiB of HBM per device.

v0:
```python
import jax
import jax.numpy as jnp
from jax import lax
from jax.sharding import PartitionSpec as P

HD = 72
SPLIT = 4
TB = 2
TILE = 16
EPS = 1e-06


def temporal(qkv_cols, dattn_cols, keep_cols, block_mask, frames):
    videos, per_owner, owners, _ = qkv_cols.shape
    band_count = owners // frames
    heads_n = dattn_cols.shape[-1] // HD
    scale = HD ** (-0.5)
    parts = qkv_cols.reshape(videos, per_owner, frames, band_count, 3, heads_n, HD)
    queries = parts[:, :, :, :, 0]
    key_part = parts[:, :, :, :, 1]
    val_part = parts[:, :, :, :, 2]
    d_out = dattn_cols.reshape(videos, per_owner, frames, band_count, heads_n, HD)
    frame_block = jnp.arange(frames) // TB
    blocks = jnp.repeat(jnp.repeat(block_mask, TB, 1), TB, 2) > 0
    same_block = frame_block[:, None] == frame_block[None, :]
    block_allow = blocks | same_block[None]
    kept = jnp.transpose(keep_cols.reshape(videos, per_owner, frames, band_count) > 0, (0, 1, 3, 2))
    diag_one = jnp.arange(frames)[:, None] == jnp.arange(frames)[None, :]
    allow = block_allow[:, None, None, None, :, :] & (kept[:, :, :, None, None, :] | diag_one)
    scores = (
        jnp.einsum("vrfshd,vrgshd->vrshfg", queries, key_part, preferred_element_type=jnp.float32)
        * scale
    )
    scores = jnp.where(allow, scores, -1e30)
    row_top = jnp.max(scores, -1, keepdims=True)
    expo = jnp.exp(scores - row_top)
    probs = expo / jnp.sum(expo, -1, keepdims=True)
    probs_b = probs.astype(jnp.bfloat16)
    attn = jnp.einsum(
        "vrshfg,vrgshd->vrfshd", probs_b, val_part, preferred_element_type=jnp.float32
    ).astype(jnp.bfloat16)
    dprob = jnp.einsum("vrfshd,vrgshd->vrshfg", d_out, val_part, preferred_element_type=jnp.float32)
    dscore = probs * (dprob - jnp.sum(probs * dprob, -1, keepdims=True))
    dscore_b = dscore.astype(jnp.bfloat16)
    grad_query = (
        jnp.einsum("vrshfg,vrgshd->vrfshd", dscore_b, key_part, preferred_element_type=jnp.float32)
        * scale
    ).astype(jnp.bfloat16)
    grad_key = (
        jnp.einsum("vrshfg,vrfshd->vrgshd", dscore_b, queries, preferred_element_type=jnp.float32)
        * scale
    ).astype(jnp.bfloat16)
    grad_value = jnp.einsum(
        "vrshfg,vrfshd->vrgshd", probs_b, d_out, preferred_element_type=jnp.float32
    ).astype(jnp.bfloat16)
    d_qkv = jnp.stack([grad_query, grad_key, grad_value], axis=4).reshape(
        videos, per_owner, owners, -1
    )
    return (attn.reshape(videos, per_owner, owners, -1), d_qkv)


def per_device(tokens, norm_gain, w_qkv, w_out, block_mask, keep_tiles, cotangent):
    owners = lax.axis_size("tm")
    videos, band_len, model_width = tokens.shape
    per_owner = band_len // owners
    frames = owners // SPLIT
    qkv_full, out_full = (
        lax.all_gather(w_qkv, "tm", axis=0, tiled=True),
        lax.all_gather(w_out, "tm", axis=0, tiled=True),
    )
    tok_float = tokens.astype(jnp.float32)
    inv_rms = lax.rsqrt(jnp.mean(tok_float * tok_float, -1, keepdims=True) + EPS)
    normed = tok_float * inv_rms
    hidden = (normed * norm_gain).astype(jnp.bfloat16)
    keep_tok = jnp.repeat(keep_tiles, TILE, axis=1).reshape(videos, per_owner, owners)
    qkv = jnp.dot(hidden, qkv_full, preferred_element_type=jnp.float32).astype(jnp.bfloat16)
    d_attn = jnp.dot(cotangent, out_full, preferred_element_type=jnp.float32).astype(jnp.bfloat16)
    qkv_cols, dattn_cols, keep_cols = (
        lax.all_to_all(
            qkv.reshape(videos, per_owner, owners, -1),
            "tm",
            split_axis=2,
            concat_axis=2,
            tiled=True,
        ),
        lax.all_to_all(
            d_attn.reshape(videos, per_owner, owners, -1),
            "tm",
            split_axis=2,
            concat_axis=2,
            tiled=True,
        ),
        lax.all_to_all(keep_tok, "tm", split_axis=2, concat_axis=2, tiled=True),
    )
    attn_cols, dqkv_cols = temporal(qkv_cols, dattn_cols, keep_cols, block_mask, frames)
    attn_rows, dqkv_rows = (
        lax.all_to_all(attn_cols, "tm", split_axis=2, concat_axis=2, tiled=True),
        lax.all_to_all(dqkv_cols, "tm", split_axis=2, concat_axis=2, tiled=True),
    )
    attn = attn_rows.reshape(videos, band_len, -1)
    d_qkv = dqkv_rows.reshape(videos, band_len, -1)
    part_qkv = jnp.einsum("vtd,vte->de", hidden, d_qkv, preferred_element_type=jnp.float32)
    part_out = jnp.einsum("vtd,vte->de", cotangent, attn, preferred_element_type=jnp.float32)
    d_hidden = lax.optimization_barrier(
        jnp.einsum("vte,de->vtd", d_qkv, qkv_full, preferred_element_type=jnp.float32).astype(
            jnp.bfloat16
        )
    )
    grad_qkv, grad_out = (
        lax.psum_scatter(part_qkv, "tm", scatter_dimension=0, tiled=True),
        lax.psum_scatter(part_out, "tm", scatter_dimension=0, tiled=True),
    )
    mixed = (
        tok_float + jnp.einsum("vte,de->vtd", attn, out_full, preferred_element_type=jnp.float32)
    ).astype(jnp.bfloat16)
    grad = d_hidden.astype(jnp.float32) * norm_gain
    grad_tokens = cotangent.astype(jnp.float32) + inv_rms * (
        grad - normed * jnp.mean(grad * normed, -1, keepdims=True)
    )
    return (mixed, grad_tokens.astype(jnp.bfloat16), grad_qkv, grad_out)


def solution(mesh):
    placed = (
        P("groups", "tm", None),
        P(),
        P("tm", None),
        P("tm", None),
        P("groups", None, None),
        P("groups", "tm"),
        P("groups", "tm", None),
    )
    return jax.shard_map(
        per_device,
        mesh=mesh,
        in_specs=placed,
        out_specs=(
            P("groups", "tm", None),
            P("groups", "tm", None),
            P(("groups", "tm"), None),
            P(("groups", "tm"), None),
        ),
        check_vma=False,
    )
```

profile of v0, /device:TPU:0, one launch (start us, length us, event | category | flops | bytes accessed | tf_op | source)
XLA Modules:
  0.0 400.1 jit_solution(6253478221850050072)
XLA Ops:
  7.2 0.7 all-gather.5.cloned.1.call-update
  7.9 0.7 all-gather.3.cloned.1.call-update
  8.6 1.3 broadcast_in_dim.16
  9.9 7.4 %all-to-all-start.1 = ((s32[1,16,16]{1,0,2:T(1,128)}), s32[1,16,16]{1,0,2:T(1,128)S(1)}, u32[]{:S(2)}, u32[]{:S(2)}) async-start(s32[1,16,16]{1,0,2:T(1,128)} %broadcast_in_dim.16), calls=%async_computation.1 | async-start | bytes 16384 | tf_op jit(solution)/shard_map/all_to_all | solution.py:93
  17.3 1.3 fusion.22
  18.6 33.7 %all-gather.5.cloned.1.call-done = bf16[1152,576]{1,0:T(8,128)(2,1)} async-done(((bf16[72,576]{1,0:T(8,128)(2,1)}), bf16[1152,576]{1,0:T(8,128)(2,1)}) %all-gather.5.cloned.1.call-update) | async-done | bytes 1327120 | tf_op jit(solution)/shard_map/all_gather | solution.py:69
  52.2 2.3 convolution_convert_fusion.4
  54.7 0.8 copy.64
  55.5 3.5 all-to-all-start.3
  59.1 48.6 %all-gather.3.cloned.1.call-done = bf16[1152,1728]{1,0:T(8,128)(2,1)} async-done(((bf16[72,1728]{1,0:T(8,128)(2,1)}), bf16[1152,1728]{1,0:T(8,128)(2,1)}) %all-gather.3.cloned.1.call-update) | async-done | bytes 3981328 | tf_op jit(solution)/shard_map/all_gather | solution.py:68
  107.7 4.0 convolution_convert_fusion.1
  111.7 0.6 copy.50
  112.3 1.3 copy.51
  113.6 3.9 all-to-all-start
  118.0 0.8 or_and_fusion
  118.7 1.3 reshape.295
  120.1 18.1 %all-to-all-done = bf16[1,16,16,1728]{3,1,0,2:T(8,128)(2,1)S(1)} async-done(((bf16[1,16,16,1728]{3,1,0,2:T(8,128)(2,1)}), bf16[1,16,16,1728]{3,1,0,2:T(8,128)(2,1)S(1)}, u32[]{:S(2)}, u32[]{:S(2)}) %all-to-all-start) | async-done | bytes 884768 | tf_op jit(solution)/shard_map/all_to_all | solution.py:79
  138.2 1.7 reshape.294
  139.9 1.4 fusion.34
  141.4 3.1 fusion.35
  144.5 0.9 fusion.14
  145.6 1.4 multiply_reduce_fusion
  147.0 0.6 multiply_convert_fusion
  147.7 0.4 copy-done.6
  148.1 0.8 fusion.12
  148.8 1.7 fusion.13
  150.6 1.1 reshape.289
  151.7 6.1 %all-to-all-start.2 = ((bf16[1,16,16,576]{3,1,0,2:T(8,128)(2,1)}), bf16[1,16,16,576]{3,1,0,2:T(8,128)(2,1)S(1)}, u32[]{:S(2)}, u32[]{:S(2)}) async-start(bf16[1,16,16,576]{3,1,0,2:T(8,128)(2,1)} %reshape.289), calls=%async_computation.2 | async-start | bytes 655360 | tf_op jit(solution)/shard_map/all_to_all | solution.py:97
  157.8 1.8 fusion.15
  159.6 1.5 pad_maximum_fusion
  161.1 0.3 copy.76
  161.4 1.9 reshape.290
  163.3 5.6 %all-to-all-done.2 = bf16[1,16,16,576]{3,1,0,2:T(8,128)(2,1)S(1)} async-done(((bf16[1,16,16,576]{3,1,0,2:T(8,128)(2,1)}), bf16[1,16,16,576]{3,1,0,2:T(8,128)(2,1)S(1)}, u32[]{:S(2)}, u32[]{:S(2)}) %all-to-all-start.2) | async-done | bytes 294944 | tf_op jit(solution)/shard_map/all_to_all | solution.py:97
  168.9 3.6 all-to-all-start.4
  172.7 2.0 convolution_bitcast_fusion
  174.8 23.5 %all-to-all-done.4 = bf16[1,16,16,1728]{3,1,0,2:T(8,128)(2,1)S(1)} async-done(((bf16[1,16,16,1728]{3,1,0,2:T(8,128)(2,1)}), bf16[1,16,16,1728]{3,1,0,2:T(8,128)(2,1)S(1)}, u32[]{:S(2)}, u32[]{:S(2)}) %all-to-all-start.4) | async-done | bytes 884768 | tf_op jit(solution)/shard_map/all_to_all | solution.py:98
  198.6 1.0 copy-done.3
  199.5 4.6 %fusion.31 = f32[1152,1728]{1,0:T(8,128)} fusion(bf16[256,1728]{1,0:T(8,128)(2,1)S(1)} %bitcast.103, bf16[1,256,1152]{2,1,0:T(8,128)(2,1)S(1)} %copy-done, f32[1152]{0:T(1024)S(1)} %copy-done.10, f32[256]{0:T(256)S(1)} %add_rsqrt_fusion), kind=kOutput, calls=%fused_computation.51 | convolution fusion | flops 1020395520 | bytes 9442816 | tf_op jit(solution)/shard_map/vtd,vte->de/dot_general | solution.py:102
  204.1 0.6 copy-done.12
  204.8 0.6 dynamic-slice
  206.0 1.5 fusion.2
  207.5 3.6 fusion.3
  211.1 0.3 fusion.17
  211.4 1.2 fusion.21
  212.7 73.5 %all-reduce.3.cloned.1.call-done = f32[1152,576]{0,1:T(8,128)} async-done(((f32[1152,576]{0,1:T(8,128)}), f32[1152,576]{0,1:T(8,128)}) %all-reduce.3.cloned.1.call-update) | async-done | bytes 2654224
  286.1 1.2 constant_dynamic-slice_fusion
  287.3 0.8 copy.72
  288.2 105.4 %reduce-scatter.3.cloned.1.call-done = f32[72,1728]{1,0:T(8,128)} async-done(((f32[1152,1728]{1,0:T(8,128)}), f32[72,1728]{1,0:T(8,128)}) %reduce-scatter.3.cloned.1.call-update) | async-done | bytes 497680 | tf_op jit(solution)/shard_map/reduce_scatter | solution.py:110
  (47 shorter events, 1.5 us)
Async XLA Ops:
  7.2 45.1 %all-gather.5.cloned.1.call-start = ((), (), s32[]{:S(2)}) async-start(), calls=%async_computation.7 | async-start | bytes 1566720 | tf_op jit(solution)/shard_map/all_gather | solution.py:69
  7.9 99.8 %all-gather.3.cloned.1.call-start = ((), (), s32[]{:S(2)}) async-start(), calls=%async_computation.6 | async-start | bytes 4386816 | tf_op jit(solution)/shard_map/all_gather | solution.py:68
  9.9 45.6 %all-to-all-start.1 = ((s32[1,16,16]{1,0,2:T(1,128)}), s32[1,16,16]{1,0,2:T(1,128)S(1)}, u32[]{:S(2)}, u32[]{:S(2)}) async-start(s32[1,16,16]{1,0,2:T(1,128)} %broadcast_in_dim.16), calls=%async_computation.1 | async-start | bytes 16384 | tf_op jit(solution)/shard_map/all_to_all | solution.py:93
  54.5 53.2 %copy-start = (bf16[1,256,1152]{2,1,0:T(8,128)(2,1)S(1)}, bf16[1,256,1152]{2,1,0:T(8,128)(2,1)}, u32[]{:S(2)}) copy-start(bf16[1,256,1152]{2,1,0:T(8,128)(2,1)} %param.7) | copy-start | bytes 1769476
  54.5 53.2 %copy-start.10 = (f32[1152]{0:T(1024)S(1)}, f32[1152]{0:T(1024)}, u32[]{:S(2)}) copy-start(f32[1152]{0:T(1024)} %param.8) | copy-start | bytes 13828
  55.5 58.1 %all-to-all-start.3 = ((bf16[1,16,16,576]{3,1,0,2:T(8,128)(2,1)}), bf16[1,16,16,576]{3,1,0,2:T(8,128)(2,1)S(1)}, u32[]{:S(2)}, u32[]{:S(2)}) async-start(bf16[1,16,16,576]{3,1,0,2:T(8,128)(2,1)} %copy.64), calls=%async_computation.3 | async-start | bytes 655360 | tf_op jit(solution)/shard_map/all_to_all | solution.py:86
  113.6 4.0 copy-start.11
  113.6 24.5 %all-to-all-start = ((bf16[1,16,16,1728]{3,1,0,2:T(8,128)(2,1)}), bf16[1,16,16,1728]{3,1,0,2:T(8,128)(2,1)S(1)}, u32[]{:S(2)}, u32[]{:S(2)}) async-start(bf16[1,16,16,1728]{3,1,0,2:T(8,128)(2,1)} %copy.51), calls=%async_computation | async-start | bytes 1835008 | tf_op jit(solution)/shard_map/all_to_all | solution.py:79
  141.4 3.1 copy-start.8
  144.4 2.6 copy-start.9
  144.4 1.1 copy-start.5
  147.0 1.0 copy-start.6
  151.7 17.2 %all-to-all-start.2 = ((bf16[1,16,16,576]{3,1,0,2:T(8,128)(2,1)}), bf16[1,16,16,576]{3,1,0,2:T(8,128)(2,1)S(1)}, u32[]{:S(2)}, u32[]{:S(2)}) async-start(bf16[1,16,16,576]{3,1,0,2:T(8,128)(2,1)} %reshape.289), calls=%async_computation.2 | async-start | bytes 655360 | tf_op jit(solution)/shard_map/all_to_all | solution.py:97
  157.8 1.8 copy-start.7
  163.3 9.4 %copy-start.2 = (bf16[1,256,1152]{2,1,0:T(8,128)(2,1)S(1)}, bf16[1,256,1152]{2,1,0:T(8,128)(2,1)}, u32[]{:S(2)}) copy-start(bf16[1,256,1152]{2,1,0:T(8,128)(2,1)} %param.13) | copy-start | bytes 1769476
  168.9 29.4 %all-to-all-start.4 = ((bf16[1,16,16,1728]{3,1,0,2:T(8,128)(2,1)}), bf16[1,16,16,1728]{3,1,0,2:T(8,128)(2,1)S(1)}, u32[]{:S(2)}, u32[]{:S(2)}) async-start(bf16[1,16,16,1728]{3,1,0,2:T(8,128)(2,1)} %reshape.290), calls=%async_computation.4 | async-start | bytes 1835008 | tf_op jit(solution)/shard_map/all_to_all | solution.py:98
  172.6 113.6 %all-reduce.3.cloned.1.call-start = ((), (), s32[]{:S(2)}) async-start(), calls=%async_computation.9 | async-start | bytes 5308416
  174.8 218.8 %reduce-scatter.3.cloned.1.call-start = ((), (), s32[]{:S(2)}) async-start(), calls=%async_computation.8 | async-start | bytes 8773632 | tf_op jit(solution)/shard_map/reduce_scatter | solution.py:110
  198.6 1.0 copy-start.3
  204.1 0.7 copy-start.12
  204.1 1.9 copy-start.1
  206.0 1.5 copy-start.4
Sparse Core Ops, SparseCore 0:
  10.1 42.0 all-gather.4
  54.5 53.1 all-gather.2
  177.0 109.1 all-reduce.2
  290.6 102.8 reduce-scatter.2
where the time goes:
time: 401 us; the launch traced here: 400 us
  waiting for transfers between devices  310 us (77%)
  matrix products  27.5 us (7%)
  starting transfers between devices  24.8 us (6%)
  local copies, waits for them, and re-layouts  17.5 us (4%)
  between operations  14.7 us (4%)
  other arithmetic  5.81 us (1%)
    reduce_scatter x1, waiting for transfers between devices, per_device(): lax.psum_scatter(part_qkv, 'tm', scatter_dimension=0, tiled=True)  105 us
    unnamed x5, waiting for transfers between devices  74.9 us
    all_gather x1, waiting for transfers between devices, per_device(): lax.all_gather(w_qkv, 'tm', axis=0, tiled=True)  48.6 us
    all_gather x1, waiting for transfers between devices, per_device(): lax.all_gather(w_out, 'tm', axis=0, tiled=True)  33.7 us
    all_to_all x1, waiting for transfers between devices, per_device(): lax.all_to_all(dqkv_cols, 'tm', split_axis=2, concat_axis=2, tiled=True)  23.5 us
    all_to_all x1, waiting for transfers between devices, per_device(): lax.all_to_all(qkv.reshape(videos, per_owner, owners, -1), 'tm', split_ax...  18.1 us
  transfers between devices with their start and end apart: 9, of which 7 were waited for; matrix products, arithmetic and copies ran while one was open for 9% of the time, Pallas kernels for 0%

commit v1 on v0

--- a/solution.py
+++ b/solution.py
@@ -8,6 +8,29 @@
 TB = 2
 TILE = 16
 EPS = 1e-06
+
+
+def cut_along(x, dim, size):
+    before, after = (x.shape[:dim], x.shape[dim + 1 :])
+    return jnp.moveaxis(x.reshape(*before, size, -1, *after), dim, 0)
+
+
+def laid_out(blocks, dim):
+    shape = list(blocks.shape[1:])
+    shape[dim] *= blocks.shape[0]
+    return jnp.moveaxis(blocks, 0, dim).reshape(shape)
+
+
+def sent_to_each(x, axis, split_dim, concat_dim):
+    count, place = (lax.axis_size(axis), lax.axis_index(axis))
+    pieces = cut_along(x, split_dim, count)
+    filled = pieces
+    for lap in range(1, count):
+        target, source = ((place + lap) % count, (place - lap) % count)
+        sent = lax.dynamic_index_in_dim(pieces, target, 0)
+        other = lax.ppermute(sent, axis, [(i, (i + lap) % count) for i in range(count)])
+        filled = lax.dynamic_update_slice_in_dim(filled, other, source, axis=0)
+    return laid_out(filled, concat_dim)
 
 
 def temporal(qkv_cols, dattn_cols, keep_cols, block_mask, frames):
@@ -95,7 +118,7 @@
     attn_cols, dqkv_cols = temporal(qkv_cols, dattn_cols, keep_cols, block_mask, frames)
     attn_rows, dqkv_rows = (
         lax.all_to_all(attn_cols, "tm", split_axis=2, concat_axis=2, tiled=True),
-        lax.all_to_all(dqkv_cols, "tm", split_axis=2, concat_axis=2, tiled=True),
+        sent_to_each(dqkv_cols, "tm", 2, 2),
     )
     attn = attn_rows.reshape(videos, band_len, -1)
     d_qkv = dqkv_rows.reshape(videos, band_len, -1)

time: 401 us -> 411 us (1.025)
  waiting for transfers between devices: 310 us -> 265 us
  local copies, waits for them, and re-layouts: 17.5 us -> 55.7 us
  starting transfers between devices: 24.8 us -> 40.5 us
    unnamed x5, waiting for transfers between devices: 74.9 us -> 17 us
    ppermute x0 -> x15, waiting for transfers between devices: none -> 35.8 us  [sent_to_each(): lax.ppermute(sent, axis, [(i, (i + lap) % count) for i in range(count)])]
    dynamic_update_slice x0 -> x15, local copies, waits for them, and re-layouts: none -> 35.1 us  [sent_to_each(): filled = lax.dynamic_update_slice_in_dim(filled, other, source, axis=0)]
    all_to_all x1 -> x0, waiting for transfers between devices: 23.5 us -> none  [per_device(): lax.all_to_all(dqkv_cols, 'tm', split_axis=2, concat_axis=2, tiled=True)]
    ppermute x0 -> x15, starting transfers between devices: none -> 19.3 us  [sent_to_each(): lax.ppermute(sent, axis, [(i, (i + lap) % count) for i in range(count)])]
  transfers between devices with their start and end apart: 9 -> 23, of which waited for: 7 -> 13; matrix products, arithmetic and copies ran while one was open for 9% -> 18% of each run, Pallas kernels for 0% -> 0%
where the time goes in v1:
time: 411 us; the launch traced here: 410 us
  waiting for transfers between devices  265 us (64%)
  local copies, waits for them, and re-layouts  55.7 us (14%)
  starting transfers between devices  40.5 us (10%)
  matrix products  26.7 us (6%)
  between operations  15.2 us (4%)
  other arithmetic  6.83 us (2%)
    reduce_scatter x1, waiting for transfers between devices, per_device(): lax.psum_scatter(part_qkv, 'tm', scatter_dimension=0, tiled=True)  105 us
    all_gather x1, waiting for transfers between devices, per_device(): lax.all_gather(w_qkv, 'tm', axis=0, tiled=True)  48.6 us
    ppermute x15, waiting for transfers between devices, sent_to_each(): lax.ppermute(sent, axis, [(i, (i + lap) % count) for i in range(count)])  35.8 us
    dynamic_update_slice x15, local copies, waits for them, and re-layouts, sent_to_each(): filled = lax.dynamic_update_slice_in_dim(filled, other, source, axis=0)  35.1 us
    all_gather x1, waiting for transfers between devices, per_device(): lax.all_gather(w_out, 'tm', axis=0, tiled=True)  33.7 us
    ppermute x15, starting transfers between devices, sent_to_each(): lax.ppermute(sent, axis, [(i, (i + lap) % count) for i in range(count)])  19.3 us
    all_to_all x1, waiting for transfers between devices, per_device(): lax.all_to_all(qkv.reshape(videos, per_owner, owners, -1), 'tm', split_ax...  18 us
    unnamed x5, waiting for transfers between devices  17 us
  transfers between devices with their start and end apart: 23, of which 13 were waited for; matrix products, arithmetic and copies ran while one was open for 18% of the time, Pallas kernels for 0%

profile of v1, /device:TPU:0, one launch (start us, length us, event | category | flops | bytes accessed | tf_op | source)
XLA Modules:
  0.0 409.6 jit_solution(15881253793933997631)
XLA Ops:
  9.9 7.4 %all-to-all-start.1 = ((s32[1,16,16]{1,0,2:T(1,128)}), s32[1,16,16]{1,0,2:T(1,128)S(1)}, u32[]{:S(2)}, u32[]{:S(2)}) async-start(s32[1,16,16]{1,0,2:T(1,128)} %broadcast_in_dim.16), calls=%async_computation.1 | async-start | bytes 16384 | tf_op jit(solution)/shard_map/all_to_all | solution.py:116
  18.6 33.7 %all-gather.5.cloned.1.call-done = bf16[1152,576]{1,0:T(8,128)(2,1)} async-done(((bf16[72,576]{1,0:T(8,128)(2,1)}), bf16[1152,576]{1,0:T(8,128)(2,1)}) %all-gather.5.cloned.1.call-update) | async-done | bytes 1327120 | tf_op jit(solution)/shard_map/all_gather | solution.py:92
  52.2 2.3 convolution_convert_fusion.4
  55.5 3.5 all-to-all-start.3
  59.1 48.6 %all-gather.3.cloned.1.call-done = bf16[1152,1728]{1,0:T(8,128)(2,1)} async-done(((bf16[72,1728]{1,0:T(8,128)(2,1)}), bf16[1152,1728]{1,0:T(8,128)(2,1)}) %all-gather.3.cloned.1.call-update) | async-done | bytes 3981328 | tf_op jit(solution)/shard_map/all_gather | solution.py:91
  107.7 4.0 convolution_convert_fusion.1
  113.6 3.8 all-to-all-start
  120.2 18.0 %all-to-all-done = bf16[1,16,16,1728]{3,1,0,2:T(8,128)(2,1)S(1)} async-done(((bf16[1,16,16,1728]{3,1,0,2:T(8,128)(2,1)}), bf16[1,16,16,1728]{3,1,0,2:T(8,128)(2,1)S(1)}, u32[]{:S(2)}, u32[]{:S(2)}) %all-to-all-start) | async-done | bytes 884768 | tf_op jit(solution)/shard_map/all_to_all | solution.py:102
  138.2 1.7 reshape.303
  139.9 1.4 fusion.34
  141.4 3.2 fusion.35
  146.7 6.1 %all-to-all-start.2 = ((bf16[1,16,16,576]{3,1,0,2:T(8,128)(2,1)}), bf16[1,16,16,576]{3,1,0,2:T(8,128)(2,1)S(1)}, u32[]{:S(2)}, u32[]{:S(2)}) async-start(bf16[1,16,16,576]{3,1,0,2:T(8,128)(2,1)} %reshape.299), calls=%async_computation.2 | async-start | bytes 655360 | tf_op jit(solution)/shard_map/all_to_all | solution.py:120
  154.5 1.6 fusion.15
  156.0 1.7 multiply_convert_fusion
  157.7 6.2 %all-to-all-done.2 = bf16[1,16,16,576]{3,1,0,2:T(8,128)(2,1)S(1)} async-done(((bf16[1,16,16,576]{3,1,0,2:T(8,128)(2,1)}), bf16[1,16,16,576]{3,1,0,2:T(8,128)(2,1)S(1)}, u32[]{:S(2)}, u32[]{:S(2)}) %all-to-all-start.2) | async-done | bytes 294944 | tf_op jit(solution)/shard_map/all_to_all | solution.py:120
  164.0 2.1 convolution_bitcast_fusion
  168.9 1.5 pad_maximum_fusion
  171.9 2.9 dynamic-slice_bitcast_fusion
  175.2 2.1 collective-permute-start.8
  177.9 1.6 collective-permute-start.6
  179.5 3.0 collective-permute-start.5
  183.8 2.0 collective-permute-start.4
  187.0 8.9 %collective-permute-start.3 = (bf16[1,1,16,1,1728]{4,0,2,3,1:T(2,128)(2,1)S(1)}, bf16[1,1,16,1,1728]{4,0,2,3,1:T(2,128)(2,1)S(1)}, u32[]{:S(2)}, u32[]{:S(2)}) collective-permute-start(bf16[1,1,16,1,1728]{4,0,2,3,1:T(2,128)(2,1)S(1)} %get-tuple-element.34), channel_id=1, source_target_pairs={{0,4},{1,5},{2,6},{3,7},{4,8},{5,9},{6,10},{7,11},{8,12},{9,13},{1... | collective-permute-start | bytes 165896 | tf_op jit(solution)/shard_map/ppermute | solution.py:31
  195.9 14.3 %collective-permute-done.7 = bf16[1,1,16,1,1728]{4,0,2,3,1:T(2,128)(2,1)S(1)} collective-permute-done((bf16[1,1,16,1,1728]{4,0,2,3,1:T(2,128)(2,1)S(1)}, bf16[1,1,16,1,1728]{4,0,2,3,1:T(2,128)(2,1)S(1)}, u32[]{:S(2)}, u32[]{:S(2)}) %collective-permute-start.7) | collective-permute-done | bytes 55328 | tf_op jit(solution)/shard_map/ppermute | solution.py:31
  210.3 3.6 collective-permute-done.6
  213.9 7.9 %collective-permute-done.5 = bf16[1,1,16,1,1728]{4,0,2,3,1:T(2,128)(2,1)S(1)} collective-permute-done((bf16[1,1,16,1,1728]{4,0,2,3,1:T(2,128)(2,1)S(1)}, bf16[1,1,16,1,1728]{4,0,2,3,1:T(2,128)(2,1)S(1)}, u32[]{:S(2)}, u32[]{:S(2)}) %collective-permute-start.5) | collective-permute-done | bytes 55328 | tf_op jit(solution)/shard_map/ppermute | solution.py:31
  221.8 3.2 collective-permute-done.4
  225.9 4.0 collective-permute-done
  230.6 2.9 dynamic_update_slice.45
  233.6 2.3 dynamic_update_slice.46
  235.9 2.3 dynamic_update_slice.47
  238.2 2.3 dynamic_update_slice.48
  240.5 2.3 dynamic_update_slice.49
  242.8 2.3 dynamic_update_slice.50
  245.1 2.3 dynamic_update_slice.51
  247.4 2.3 dynamic_update_slice.52
  249.7 2.3 dynamic_update_slice.53
  252.0 2.3 dynamic_update_slice.54
  254.3 2.3 dynamic_update_slice.55
  256.6 2.3 dynamic_update_slice.56
  259.0 2.3 dynamic_update_slice.57
  261.3 2.3 dynamic_update_slice.58
  263.6 2.3 dynamic_update_slice.59
  265.9 4.6 %fusion.31 = f32[1152,1728]{1,0:T(8,128)} fusion(bf16[256,1728]{1,0:T(8,128)(2,1)S(1)} %bitcast.135, bf16[1,256,1152]{2,1,0:T(8,128)(2,1)S(1)} %copy-done, f32[1152]{0:T(1024)S(1)} %copy-done.11, f32[256]{0:T(256)S(1)} %add_rsqrt_fusion), kind=kOutput, calls=%fused_computation.51 | convolution fusion | flops 1020395520 | bytes 9442816 | tf_op jit(solution)/shard_map/vtd,vte->de/dot_general | solution.py:125
  272.4 3.6 fusion.3
  278.6 1.5 fusion.2
  280.1 15.6 %all-reduce.3.cloned.1.call-done = f32[1152,576]{0,1:T(8,128)} async-done(((f32[1152,576]{0,1:T(8,128)}), f32[1152,576]{0,1:T(8,128)}) %all-reduce.3.cloned.1.call-update) | async-done | bytes 2654224
  297.7 105.4 %reduce-scatter.3.cloned.1.call-done = f32[72,1728]{1,0:T(8,128)} async-done(((f32[1152,1728]{1,0:T(8,128)}), f32[72,1728]{1,0:T(8,128)}) %reduce-scatter.3.cloned.1.call-update) | async-done | bytes 497680 | tf_op jit(solution)/shard_map/reduce_scatter | solution.py:133
  (96 shorter events, 28.3 us)
Async XLA Ops:
  7.2 45.1 %all-gather.5.cloned.1.call-start = ((), (), s32[]{:S(2)}) async-start(), calls=%async_computation.6 | async-start | bytes 1566720 | tf_op jit(solution)/shard_map/all_gather | solution.py:92
  7.9 99.8 %all-gather.3.cloned.1.call-start = ((), (), s32[]{:S(2)}) async-start(), calls=%async_computation.5 | async-start | bytes 4386816 | tf_op jit(solution)/shard_map/all_gather | solution.py:91
  9.9 45.6 %all-to-all-start.1 = ((s32[1,16,16]{1,0,2:T(1,128)}), s32[1,16,16]{1,0,2:T(1,128)S(1)}, u32[]{:S(2)}, u32[]{:S(2)}) async-start(s32[1,16,16]{1,0,2:T(1,128)} %broadcast_in_dim.16), calls=%async_computation.1 | async-start | bytes 16384 | tf_op jit(solution)/shard_map/all_to_all | solution.py:116
  54.5 53.2 %copy-start = (bf16[1,256,1152]{2,1,0:T(8,128)(2,1)S(1)}, bf16[1,256,1152]{2,1,0:T(8,128)(2,1)}, u32[]{:S(2)}) copy-start(bf16[1,256,1152]{2,1,0:T(8,128)(2,1)} %param.7) | copy-start | bytes 1769476
  54.5 53.2 %copy-start.11 = (f32[1152]{0:T(1024)S(1)}, f32[1152]{0:T(1024)}, u32[]{:S(2)}) copy-start(f32[1152]{0:T(1024)} %param.8) | copy-start | bytes 13828
  55.5 58.1 %all-to-all-start.3 = ((bf16[1,16,16,576]{3,1,0,2:T(8,128)(2,1)}), bf16[1,16,16,576]{3,1,0,2:T(8,128)(2,1)S(1)}, u32[]{:S(2)}, u32[]{:S(2)}) async-start(bf16[1,16,16,576]{3,1,0,2:T(8,128)(2,1)} %copy.63), calls=%async_computation.3 | async-start | bytes 655360 | tf_op jit(solution)/shard_map/all_to_all | solution.py:109
  113.6 4.0 copy-start.14
  113.6 24.5 %all-to-all-start = ((bf16[1,16,16,1728]{3,1,0,2:T(8,128)(2,1)}), bf16[1,16,16,1728]{3,1,0,2:T(8,128)(2,1)S(1)}, u32[]{:S(2)}, u32[]{:S(2)}) async-start(bf16[1,16,16,1728]{3,1,0,2:T(8,128)(2,1)} %copy.50), calls=%async_computation | async-start | bytes 1835008 | tf_op jit(solution)/shard_map/all_to_all | solution.py:102
  139.9 1.5 copy-start.13
  141.4 3.2 copy-start.5
  141.4 3.2 copy-start.9
  144.6 9.9 %copy-start.10 = (f32[16,4,8,4]{3,2,1,0:T(8,128)}, f32[16,4,8,4]{3,2,1,0:T(8,128)S(1)}, u32[]{:S(2)}) copy-start(f32[16,4,8,4]{3,2,1,0:T(8,128)S(1)} %get-tuple-element.38) | copy-start | bytes 24580
  145.5 7.6 %copy-start.4 = (bf16[16,4,4,8,72]{4,3,0,2,1:T(8,128)(2,1)S(1)}, bf16[16,4,4,8,72]{4,3,0,2,1:T(8,128)(2,1)}, u32[]{:S(2)}) copy-start(bf16[16,4,4,8,72]{4,3,0,2,1:T(8,128)(2,1)} %reshape.304) | copy-start | bytes 884740
  146.7 17.2 %all-to-all-start.2 = ((bf16[1,16,16,576]{3,1,0,2:T(8,128)(2,1)}), bf16[1,16,16,576]{3,1,0,2:T(8,128)(2,1)S(1)}, u32[]{:S(2)}, u32[]{:S(2)}) async-start(bf16[1,16,16,576]{3,1,0,2:T(8,128)(2,1)} %reshape.299), calls=%async_computation.2 | async-start | bytes 655360 | tf_op jit(solution)/shard_map/all_to_all | solution.py:120
  152.8 142.9 %all-reduce.3.cloned.1.call-start = ((), (), s32[]{:S(2)}) async-start(), calls=%async_computation.8 | async-start | bytes 5308416
  156.0 7.9 %copy-start.2 = (bf16[1,256,1152]{2,1,0:T(8,128)(2,1)S(1)}, bf16[1,256,1152]{2,1,0:T(8,128)(2,1)}, u32[]{:S(2)}) copy-start(bf16[1,256,1152]{2,1,0:T(8,128)(2,1)} %param.13) | copy-start | bytes 1769476
  166.1 1.0 copy-start.7
  166.1 1.8 copy-start.6
  166.1 237.0 %reduce-scatter.3.cloned.1.call-start = ((), (), s32[]{:S(2)}) async-start(), calls=%async_computation.7 | async-start | bytes 8773632 | tf_op jit(solution)/shard_map/reduce_scatter | solution.py:133
  167.9 1.0 copy-start.8
  174.8 9.0 %collective-permute-start.9 = (bf16[1,1,16,1,1728]{4,0,2,3,1:T(2,128)(2,1)S(1)}, bf16[1,1,16,1,1728]{4,0,2,3,1:T(2,128)(2,1)S(1)}, u32[]{:S(2)}, u32[]{:S(2)}) collective-permute-start(bf16[1,1,16,1,1728]{4,0,2,3,1:T(2,128)(2,1)S(1)} %get-tuple-element.28), channel_id=1, source_target_pairs={{0,10},{1,11},{2,12},{3,13},{4,14},{5,15},{6,0},{7,1},{8,2},{9,3},... | collective-permute-start | bytes 165896 | tf_op jit(solution)/shard_map/ppermute | solution.py:31
  175.2 11.8 %collective-permute-start.8 = (bf16[1,1,16,1,1728]{4,0,2,3,1:T(2,128)(2,1)S(1)}, bf16[1,1,16,1,1728]{4,0,2,3,1:T(2,128)(2,1)S(1)}, u32[]{:S(2)}, u32[]{:S(2)}) collective-permute-start(bf16[1,1,16,1,1728]{4,0,2,3,1:T(2,128)(2,1)S(1)} %get-tuple-element.29), channel_id=1, source_target_pairs={{0,9},{1,10},{2,11},{3,12},{4,13},{5,14},{6,15},{7,0},{8,1},{9,2},... | collective-permute-start | bytes 165896 | tf_op jit(solution)/shard_map/ppermute | solution.py:31
  177.3 33.0 %collective-permute-start.7 = (bf16[1,1,16,1,1728]{4,0,2,3,1:T(2,128)(2,1)S(1)}, bf16[1,1,16,1,1728]{4,0,2,3,1:T(2,128)(2,1)S(1)}, u32[]{:S(2)}, u32[]{:S(2)}) collective-permute-start(bf16[1,1,16,1,1728]{4,0,2,3,1:T(2,128)(2,1)S(1)} %get-tuple-element.30), channel_id=1, source_target_pairs={{0,8},{1,9},{2,10},{3,11},{4,12},{5,13},{6,14},{7,15},{8,0},{9,1},... | collective-permute-start | bytes 165896 | tf_op jit(solution)/shard_map/ppermute | solution.py:31
  177.9 36.0 %collective-permute-start.6 = (bf16[1,1,16,1,1728]{4,0,2,3,1:T(2,128)(2,1)S(1)}, bf16[1,1,16,1,1728]{4,0,2,3,1:T(2,128)(2,1)S(1)}, u32[]{:S(2)}, u32[]{:S(2)}) collective-permute-start(bf16[1,1,16,1,1728]{4,0,2,3,1:T(2,128)(2,1)S(1)} %get-tuple-element.31), channel_id=1, source_target_pairs={{0,7},{1,8},{2,9},{3,10},{4,11},{5,12},{6,13},{7,14},{8,15},{9,0},... | collective-permute-start | bytes 165896 | tf_op jit(solution)/shard_map/ppermute | solution.py:31
  179.5 42.4 %collective-permute-start.5 = (bf16[1,1,16,1,1728]{4,0,2,3,1:T(2,128)(2,1)S(1)}, bf16[1,1,16,1,1728]{4,0,2,3,1:T(2,128)(2,1)S(1)}, u32[]{:S(2)}, u32[]{:S(2)}) collective-permute-start(bf16[1,1,16,1,1728]{4,0,2,3,1:T(2,128)(2,1)S(1)} %get-tuple-element.32), channel_id=1, source_target_pairs={{0,6},{1,7},{2,8},{3,9},{4,10},{5,11},{6,12},{7,13},{8,14},{9,15},... | collective-permute-start | bytes 165896 | tf_op jit(solution)/shard_map/ppermute | solution.py:31
  183.8 41.3 %collective-permute-start.4 = (bf16[1,1,16,1,1728]{4,0,2,3,1:T(2,128)(2,1)S(1)}, bf16[1,1,16,1,1728]{4,0,2,3,1:T(2,128)(2,1)S(1)}, u32[]{:S(2)}, u32[]{:S(2)}) collective-permute-start(bf16[1,1,16,1,1728]{4,0,2,3,1:T(2,128)(2,1)S(1)} %get-tuple-element.33), channel_id=1, source_target_pairs={{0,5},{1,6},{2,7},{3,8},{4,9},{5,10},{6,11},{7,12},{8,13},{9,14},{... | collective-permute-start | bytes 165896 | tf_op jit(solution)/shard_map/ppermute | solution.py:31
  187.0 38.0 %collective-permute-start.3 = (bf16[1,1,16,1,1728]{4,0,2,3,1:T(2,128)(2,1)S(1)}, bf16[1,1,16,1,1728]{4,0,2,3,1:T(2,128)(2,1)S(1)}, u32[]{:S(2)}, u32[]{:S(2)}) collective-permute-start(bf16[1,1,16,1,1728]{4,0,2,3,1:T(2,128)(2,1)S(1)} %get-tuple-element.34), channel_id=1, source_target_pairs={{0,4},{1,5},{2,6},{3,7},{4,8},{5,9},{6,10},{7,11},{8,12},{9,13},{1... | collective-permute-start | bytes 165896 | tf_op jit(solution)/shard_map/ppermute | solution.py:31
  210.3 14.8 %collective-permute-start.2 = (bf16[1,1,16,1,1728]{4,0,2,3,1:T(2,128)(2,1)S(1)}, bf16[1,1,16,1,1728]{4,0,2,3,1:T(2,128)(2,1)S(1)}, u32[]{:S(2)}, u32[]{:S(2)}) collective-permute-start(bf16[1,1,16,1,1728]{4,0,2,3,1:T(2,128)(2,1)S(1)} %get-tuple-element.35), channel_id=1, source_target_pairs={{0,3},{1,4},{2,5},{3,6},{4,7},{5,8},{6,9},{7,10},{8,11},{9,12},{10... | collective-permute-start | bytes 165896 | tf_op jit(solution)/shard_map/ppermute | solution.py:31
  213.9 11.2 %collective-permute-start.1 = (bf16[1,1,16,1,1728]{4,0,2,3,1:T(2,128)(2,1)S(1)}, bf16[1,1,16,1,1728]{4,0,2,3,1:T(2,128)(2,1)S(1)}, u32[]{:S(2)}, u32[]{:S(2)}) collective-permute-start(bf16[1,1,16,1,1728]{4,0,2,3,1:T(2,128)(2,1)S(1)} %get-tuple-element.36), channel_id=1, source_target_pairs={{0,2},{1,3},{2,4},{3,5},{4,6},{5,7},{6,8},{7,9},{8,10},{9,11},{10,... | collective-permute-start | bytes 165896 | tf_op jit(solution)/shard_map/ppermute | solution.py:31
  221.8 8.1 %collective-permute-start = (bf16[1,1,16,1,1728]{4,0,2,3,1:T(2,128)(2,1)S(1)}, bf16[1,1,16,1,1728]{4,0,2,3,1:T(2,128)(2,1)S(1)}, u32[]{:S(2)}, u32[]{:S(2)}) collective-permute-start(bf16[1,1,16,1,1728]{4,0,2,3,1:T(2,128)(2,1)S(1)} %get-tuple-element.37), channel_id=1, source_target_pairs={{0,1},{1,2},{2,3},{3,4},{4,5},{5,6},{6,7},{7,8},{8,9},{9,10},{10,1... | collective-permute-start | bytes 165896 | tf_op jit(solution)/shard_map/ppermute | solution.py:31
  225.0 33.9 %collective-permute-start.12 = (bf16[1,1,16,1,1728]{4,0,2,3,1:T(2,128)(2,1)}, bf16[1,1,16,1,1728]{4,0,2,3,1:T(2,128)(2,1)S(1)}, u32[]{:S(2)}, u32[]{:S(2)}) collective-permute-start(bf16[1,1,16,1,1728]{4,0,2,3,1:T(2,128)(2,1)} %get-tuple-element.25), channel_id=1, source_target_pairs={{0,13},{1,14},{2,15},{3,0},{4,1},{5,2},{6,3},{7,4},{8,5},{9,6},{10... | collective-permute-start | bytes 165896 | tf_op jit(solution)/shard_map/ppermute | solution.py:31
  225.1 29.3 %collective-permute-start.10 = (bf16[1,1,16,1,1728]{4,0,2,3,1:T(2,128)(2,1)}, bf16[1,1,16,1,1728]{4,0,2,3,1:T(2,128)(2,1)S(1)}, u32[]{:S(2)}, u32[]{:S(2)}) collective-permute-start(bf16[1,1,16,1,1728]{4,0,2,3,1:T(2,128)(2,1)} %get-tuple-element.27), channel_id=1, source_target_pairs={{0,11},{1,12},{2,13},{3,14},{4,15},{5,0},{6,1},{7,2},{8,3},{9,4},{... | collective-permute-start | bytes 165896 | tf_op jit(solution)/shard_map/ppermute | solution.py:31
  225.1 31.6 %collective-permute-start.11 = (bf16[1,1,16,1,1728]{4,0,2,3,1:T(2,128)(2,1)}, bf16[1,1,16,1,1728]{4,0,2,3,1:T(2,128)(2,1)S(1)}, u32[]{:S(2)}, u32[]{:S(2)}) collective-permute-start(bf16[1,1,16,1,1728]{4,0,2,3,1:T(2,128)(2,1)} %get-tuple-element.26), channel_id=1, source_target_pairs={{0,12},{1,13},{2,14},{3,15},{4,0},{5,1},{6,2},{7,3},{8,4},{9,5},{1... | collective-permute-start | bytes 165896 | tf_op jit(solution)/shard_map/ppermute | solution.py:31
  225.1 36.1 %collective-permute-start.13 = (bf16[1,1,16,1,1728]{4,0,2,3,1:T(2,128)(2,1)}, bf16[1,1,16,1,1728]{4,0,2,3,1:T(2,128)(2,1)S(1)}, u32[]{:S(2)}, u32[]{:S(2)}) collective-permute-start(bf16[1,1,16,1,1728]{4,0,2,3,1:T(2,128)(2,1)} %get-tuple-element.24), channel_id=1, source_target_pairs={{0,14},{1,15},{2,0},{3,1},{4,2},{5,3},{6,4},{7,5},{8,6},{9,7},{10,... | collective-permute-start | bytes 165896 | tf_op jit(solution)/shard_map/ppermute | solution.py:31
  230.0 0.6 copy-start.12
  230.6 33.0 %collective-permute-start.14 = (bf16[1,1,16,1,1728]{4,0,2,3,1:T(2,128)(2,1)}, bf16[1,1,16,1,1728]{4,0,2,3,1:T(2,128)(2,1)S(1)}, u32[]{:S(2)}, u32[]{:S(2)}) collective-permute-start(bf16[1,1,16,1,1728]{4,0,2,3,1:T(2,128)(2,1)} %get-tuple-element.23), channel_id=1, source_target_pairs={{0,15},{1,0},{2,1},{3,2},{4,3},{5,4},{6,5},{7,6},{8,7},{9,8},{10,9... | collective-permute-start | bytes 165896 | tf_op jit(solution)/shard_map/ppermute | solution.py:31
  270.5 0.7 copy-start.15
  276.0 1.1 copy-start.3
  277.1 1.5 copy-start.1
Sparse Core Ops, SparseCore 0:
  10.1 42.0 all-gather.4
  54.5 53.1 all-gather.2
  166.2 129.4 all-reduce.2
  300.2 102.8 reduce-scatter.2
